TPU v7x, 128 devices: a whole 4x4x4 slice. The times are simulated.
128 devices in a mesh: group: 4 (over x), member: 32 (over z, y, core).
Axes of the slice: x: 4, y: 4, z: 4, core: 2. Of those that a mesh axis runs over, the one named last changes fastest.
Arguments:
- mesh_vector: bfloat16 [131072, 128], P(('group', 'member')), may hold values from -6 to 6
- cluster_position: int32 [131072], P(('group', 'member')), may hold values from 0 to 131071, as said below
- cluster_sizes: int32 [128], replicated, may hold values from 256 to 1792, as said below
- block_ranks: int32 [254], replicated, may hold values from 32 to 128, as said below
- diag_block: bfloat16 [2, 229376, 1792], P(None, ('group', 'member')), may hold values from -0.09375 to 0.09375
- top_left: bfloat16 [2, 2, 229376, 128], P(None, None, ('group', 'member')), may hold values from -0.375 to 0.375
- top_right: bfloat16 [2, 2, 229376, 128], P(None, None, ('group', 'member'))
- low_left: bfloat16 [5, 2, 229376, 64], P(None, None, ('group', 'member')), may hold values from -0.5 to 0.5
- low_right: bfloat16 [5, 2, 229376, 64], P(None, None, ('group', 'member'))
Outputs:
- product: float32 [131072, 128], P(('group', 'member'))
Inputs may be any that keep to these rules, and one draw needn't show every extreme that they name: `cluster_position`: A permutation of the unknowns. In cluster order every aligned run of 128 positions holds exactly one row of each device, so each device holds exactly size / 128 rows of every cluster. `cluster_sizes`: multiples of 128 that sum to 131072; one is exactly 1792. `block_ranks`: entries 0 .. 5 lie in 64 .. 128, the others in 32 .. 64; entry 0 is 128.
All inputs are finite; a program needn't handle non-finite values.
Results may differ from a plain program's by a relative error of at most 0.0027.
Values may be sent and summed in bfloat16 or wider, within the bound.
A program may use at most 64 MiB of HBM per device.

v0:
```python
import jax
import jax.numpy as jnp
from jax import lax
from jax.sharding import PartitionSpec as P


def partner(block, axis, apart):
    count = lax.axis_size(axis)
    route = []
    for low in range(count):
        high = low | 1 << apart
        if high != low and high < count:
            route += [(low, high), (high, low)]
    return lax.ppermute(block, axis, route)


def rotate(values):
    middle = values.shape[-1] // 2
    return jnp.concatenate([-values[..., middle:], values[..., :middle]], axis=-1)


def level_ranks(block_ranks, device, first_level, count, levels):
    picks = []
    for position in range(count):
        tree_level = first_level + position
        node_index = jnp.right_shift(device, levels - tree_level)
        picks.append(block_ranks[2**tree_level - 2 + node_index])
    return jnp.stack(picks)


def masked_pairs(coefficient, ranks):
    rank_cap = coefficient.shape[1]
    keep_mask = jnp.arange(rank_cap, dtype=jnp.int32)[None, :] < ranks[:, None]
    rounded = jnp.where(keep_mask[:, :, None], coefficient, 0.0).astype(jnp.bfloat16)
    return jnp.stack([rounded, rotate(rounded)], axis=1)


def on_device(
    mesh_vector,
    cluster_position,
    cluster_sizes,
    block_ranks,
    diag_block,
    top_left,
    top_right,
    low_left,
    low_right,
):
    groups = lax.axis_size("group")
    members = lax.axis_size("member")
    leaves = groups * members
    group_levels = groups.bit_length() - 1
    member_levels = members.bit_length() - 1
    levels = group_levels + member_levels
    device = lax.axis_index("group") * members + lax.axis_index("member")
    capacity = diag_block.shape[1]
    bucket = capacity // leaves
    columns = mesh_vector.shape[1]
    cluster_ends = jnp.cumsum(cluster_sizes)
    starts = cluster_ends - cluster_sizes
    owners = jnp.sum((cluster_position[:, None] >= cluster_ends[None, :]).astype(jnp.int32), axis=1)
    picked = owners[:, None] == jnp.arange(leaves, dtype=jnp.int32)[None, :]
    first_row = jnp.sum(jnp.where(picked, starts[None, :], 0), axis=1)
    within = cluster_position - first_row
    placing = owners * bucket + within // leaves
    outgoing = jnp.zeros((leaves * bucket, columns), mesh_vector.dtype).at[placing].set(mesh_vector)
    targets = jnp.full((leaves * bucket,), capacity, jnp.int32).at[placing].set(within)
    arrived, slot_ids = (
        lax.all_to_all(
            outgoing.reshape(leaves, bucket, columns),
            ("group", "member"),
            split_axis=0,
            concat_axis=0,
            tiled=True,
        ),
        lax.all_to_all(
            targets.reshape(leaves, bucket),
            ("group", "member"),
            split_axis=0,
            concat_axis=0,
            tiled=True,
        ),
    )
    arrived = arrived.reshape(leaves * bucket, columns)
    slot_ids = slot_ids.reshape(leaves * bucket)
    cluster_field = (
        jnp.zeros((capacity, columns), mesh_vector.dtype).at[slot_ids].set(arrived, mode="drop")
    )
    paired = jnp.stack([cluster_field, rotate(cluster_field)])
    top_part = jnp.einsum("lprk,prn->lkn", top_right, paired, preferred_element_type=jnp.float32)
    low_part = jnp.einsum("lprk,prn->lkn", low_right, paired, preferred_element_type=jnp.float32)
    result = jnp.einsum("prc,pcn->rn", diag_block, paired, preferred_element_type=jnp.float32)
    low_coefs = []
    for low_pos in range(member_levels):
        sibling_bit = member_levels - 1 - low_pos
        running = low_part[low_pos]
        for lower_bit in range(sibling_bit):
            running = running + partner(running, "member", lower_bit)
        low_coefs.append(
            partner(running.astype(jnp.bfloat16), "member", sibling_bit).astype(running.dtype)
        )
    low_coef = jnp.stack(low_coefs)
    member_summed = lax.psum(top_part, "member")
    pending = [member_summed[group_levels - 1 - group_bit] for group_bit in range(group_levels)]
    gotten = []
    for group_bit in range(group_levels):
        received = partner(jnp.stack(pending[group_bit:]), "group", group_bit)
        gotten.append(received[0])
        for pending_bit in range(group_bit + 1, group_levels):
            pending[pending_bit] = pending[pending_bit] + received[pending_bit - group_bit]
    top_coef = jnp.stack(
        [gotten[group_levels - 1 - level_pos] for level_pos in range(group_levels)]
    )
    top_ranks = level_ranks(block_ranks, device, 1, group_levels, levels)
    low_ranks = level_ranks(block_ranks, device, group_levels + 1, member_levels, levels)
    result = result + jnp.einsum(
        "lprk,lpkn->rn",
        top_left,
        masked_pairs(top_coef, top_ranks),
        preferred_element_type=jnp.float32,
    )
    result = result + jnp.einsum(
        "lprk,lpkn->rn",
        low_left,
        masked_pairs(low_coef, low_ranks),
        preferred_element_type=jnp.float32,
    )
    leaving = result[jnp.minimum(slot_ids, capacity - 1)]
    returned = lax.all_to_all(
        leaving.reshape(leaves, bucket, columns),
        ("group", "member"),
        split_axis=0,
        concat_axis=0,
        tiled=True,
    )
    returned = returned.reshape(leaves * bucket, columns)
    return returned[placing]


def solution(mesh):
    return jax.shard_map(
        on_device,
        mesh=mesh,
        in_specs=(
            P(("group", "member"), None),
            P(("group", "member")),
            P(),
            P(),
            P(None, ("group", "member"), None),
            P(None, None, ("group", "member"), None),
            P(None, None, ("group", "member"), None),
            P(None, None, ("group", "member"), None),
            P(None, None, ("group", "member"), None),
        ),
        out_specs=P(("group", "member"), None),
        check_vma=False,
    )
```

profile of v0, /device:TPU:1, one launch (start us, length us, event | category | flops | bytes accessed | tf_op | source)
XLA Modules:
  0.0 249.3 jit_solution(16727595233815144738)
XLA Ops:
  6.5 0.9 copy.33
  7.4 0.2 reduce-window.8
  7.7 0.7 sub.12
  8.4 1.0 convert_reduce_fusion
  9.4 0.4 select_reduce_fusion
  9.8 0.7 broadcast_clamp_fusion
  10.5 4.3 %scatter_custom_fusion = s32[1792]{0:T(1024)S(1)} fusion(s32[1024]{0:T(1024)S(1)} %get-tuple-element.8, s32[1024]{0:T(1024)S(1)} %get-tuple-element.9, s32[]{:T(128)} %constant.20.clone.1), kind=kCustom, calls=%fused_computation.85 | custom fusion | bytes 7172 | tf_op jit(solution)/shard_map/scatter | solution.py:67
  14.8 0.8 all_to_all.12
  15.6 11.5 %all-to-all-start = ((s32[128,1,14]{2,1,0:T(1,128)}), s32[128,1,14]{2,1,0:T(1,128)S(1)}, u32[]{:S(2)}, u32[]{:S(2)}) async-start(s32[128,1,14]{2,1,0:T(1,128)} %bitcast.1), calls=%async_computation | async-start | bytes 131072 | tf_op jit(solution)/shard_map/all_to_all | solution.py:76
  27.1 1.6 fusion.38
  28.7 1.4 pad_add_fusion
  30.2 3.7 %scatter_custom_fusion.1 = bf16[1792,128]{1,0:T(8,128)(2,1)S(1)} fusion(s32[1024]{0:T(1024)S(1)} %get-tuple-element.8, bf16[1024,128]{1,0:T(8,128)(2,1)} %param.9, bf16[]{:T(256)} %constant.19.clone.1), kind=kCustom, calls=%fused_computation.23 | custom fusion | bytes 459264 | tf_op jit(solution)/shard_map/scatter | solution.py:66
  33.8 0.9 reshape.248
  34.7 1.8 all-to-all-done
  36.6 7.9 %all-to-all-start.1 = ((bf16[128,14,128]{2,1,0:T(8,128)(2,1)}), bf16[128,14,128]{2,1,0:T(8,128)(2,1)S(1)}, u32[]{:S(2)}, u32[]{:S(2)}) async-start(bf16[128,14,128]{2,1,0:T(8,128)(2,1)} %reshape.248), calls=%async_computation.1 | async-start | bytes 1048576 | tf_op jit(solution)/shard_map/all_to_all | solution.py:69
  44.6 0.6 iota_compare_fusion.2
  45.2 3.2 %stack.83 = s32[5]{0:T(128)S(1)} concatenate(s32[1]{0:T(128)} %get-tuple-element.32, s32[1]{0:T(128)} %get-tuple-element.31, s32[1]{0:T(128)} %get-tuple-element.30, s32[1]{0:T(128)} %get-tuple-element.35, s32[1]{0:T(128)} %get-tuple-element.29), dimensions={0} | concatenate | bytes 40 | tf_op jit(solution)/shard_map/stack | solution.py:28
  48.4 0.5 broadcast.152
  49.0 0.8 reduce.8
  49.8 0.1 reshape.247
  50.0 8.0 %all-to-all-done.1 = bf16[128,14,128]{2,1,0:T(8,128)(2,1)S(1)} async-done(((bf16[128,14,128]{2,1,0:T(8,128)(2,1)}), bf16[128,14,128]{2,1,0:T(8,128)(2,1)S(1)}, u32[]{:S(2)}, u32[]{:S(2)}) %all-to-all-start.1) | async-done | bytes 458784 | tf_op jit(solution)/shard_map/all_to_all | solution.py:69
  58.0 0.9 reshape.288
  58.9 8.3 %scatter_custom_fusion.2 = bf16[1792,128]{1,0:T(8,128)(2,1)S(1)} fusion(s32[1792]{0:T(1024)S(1)} %get-tuple-element.6, bf16[1792,128]{1,0:T(8,128)(2,1)} %reshape.288, bf16[]{:T(256)} %constant.19.clone.1), kind=kCustom, calls=%fused_computation.21 | custom fusion | bytes 459264 | tf_op jit(solution)/shard_map/scatter | solution.py:87
  67.3 0.2 copy.35
  67.6 2.5 %convolution_bitcast_fusion.3 = f32[5,64,128]{2,1,0:T(8,128)S(1)} fusion(bf16[5,2,1792,64]{2,3,1,0:T(8,128)(2,1)} %param.17, bf16[1,1792,128]{1,2,0:T(8,128)(2,1)S(1)} %maximum_bitcast_fusion, bf16[1,1792,128]{1,2,0:T(8,128)(2,1)S(1)} %bitcast.109), kind=kOutput, calls=%fused_computation.11 | convolution fusion | flops 295436288 | bytes 3375104 | tf_op jit(solution)/shard_map/lprk,prn->lkn/dot_general | solution.py:91
  70.1 0.7 slice_bitcast_fusion
  70.8 0.6 fusion.23
  71.4 1.1 collective-permute-start.11
  72.5 0.5 collective-permute-start.2
  73.0 0.5 collective-permute-start.16
  73.5 1.1 convolution_bitcast_fusion.4
  74.6 9.8 %convolution_bitcast_fusion.2 = f32[128,1792]{1,0:T(8,128)} fusion(bf16[2,1792,1792]{2,1,0:T(8,128)(2,1)} %param.13, bf16[1,1792,128]{1,2,0:T(8,128)(2,1)S(1)} %maximum_bitcast_fusion, bf16[1,1792,128]{1,2,0:T(8,128)(2,1)S(1)} %bitcast.111), kind=kOutput, calls=%fused_computation.7 | convolution fusion | flops 1644625920 | bytes 14680064 | tf_op jit(solution)/shard_map/prc,pcn->rn/dot_general | solution.py:92
  84.4 0.6 copy-done.3
  85.0 0.6 copy-done.4
  85.6 0.8 add_convert_fusion
  86.4 0.2 collective-permute-start.8
  86.6 1.4 collective-permute-start.3
  88.1 1.4 collective-permute-start.15
  89.5 80.7 %all-reduce.2.cloned.1.call-done = f32[2,128,128]{1,2,0:T(8,128)} async-done(((f32[2,128,128]{1,2,0:T(8,128)}), f32[2,128,128]{1,2,0:T(8,128)}) %all-reduce.2.cloned.1.call-update) | async-done | bytes 131088 | tf_op jit(solution)/shard_map/psum | solution.py:103
  170.2 1.0 fusion.37
  171.2 2.1 collective-permute-start.4
  173.3 1.3 collective-permute-start
  174.6 1.0 collective-permute-done.4
  175.6 2.0 collective-permute-start.9
  177.7 2.7 %collective-permute-done.5 = f32[64,128]{1,0:T(8,128)S(1)} collective-permute-done((f32[64,128]{1,0:T(8,128)S(1)}, f32[64,128]{1,0:T(8,128)S(1)}, u32[]{:S(2)}, u32[]{:S(2)}) %collective-permute-start.5) | collective-permute-done | bytes 32800 | tf_op jit(solution)/shard_map/ppermute | solution.py:14
  180.4 1.0 collective-permute-start.13
  181.4 2.1 collective-permute-start.6
  183.6 2.0 collective-permute-done.6
  185.6 0.7 collective-permute-start.10
  186.3 2.2 collective-permute-done.10
  188.5 0.1 select_convert_fusion
  188.9 0.9 slice_bitcast_fusion.4
  189.8 2.8 %collective-permute-start.1 = (bf16[1,128,128]{1,2,0:T(8,128)(2,1)S(1)}, bf16[1,128,128]{1,2,0:T(8,128)(2,1)S(1)}, u32[]{:S(2)}, u32[]{:S(2)}) collective-permute-start(bf16[1,128,128]{1,2,0:T(8,128)(2,1)S(1)} %get-tuple-element.22), channel_id=1, source_target_pairs={{0,64},{64,0},{32,96},{96,32},{1,65},{65,1},{33,97},{97,33},{2,66}... | collective-permute-start | bytes 98312 | tf_op jit(solution)/shard_map/ppermute | solution.py:14
  192.7 1.5 collective-permute-done.1
  194.2 0.6 fusion.11
  194.8 0.6 fusion.10
  195.5 0.7 fusion.2
  196.2 1.5 fusion.1
  197.7 1.5 copy.41
  199.2 4.2 %gather_fusion = f32[1792,128]{1,0:T(8,128)} fusion(f32[1792,128]{1,0:T(8,128)S(1)} %copy.41, s32[2048]{0:T(1024)S(1)} %pad_clamp_fusion), kind=kCustom, calls=%fused_computation | custom fusion | bytes 1842176 | tf_op jit(solution)/shard_map/gather | solution.py:128
  203.4 1.3 reshape.250
  204.7 32.4 %all_to_all.19 = f32[128,14,128]{2,1,0:T(8,128)} all-to-all(f32[128,14,128]{2,1,0:T(8,128)S(1)} %reshape.250), channel_id=1, replica_groups=mesh['group'=4,'member'=32] {'group','member'}, dimensions={0} | all-to-all | bytes 1835008 | tf_op jit(solution)/shard_map/all_to_all | solution.py:129
  237.1 1.3 reshape.251
  238.4 4.0 %gather_fusion.1 = f32[1024,128]{1,0:T(8,128)} fusion(f32[1792,128]{1,0:T(8,128)S(1)} %reshape.251, s32[1024]{0:T(1024)S(1)} %get-tuple-element.7), kind=kCustom, calls=%fused_computation.1 | custom fusion | bytes 1052672 | tf_op jit(solution)/shard_map/gather | solution.py:137
  (56 shorter events, 1.0 us)
Async XLA Ops:
  6.5 189.7 %copy-start = (bf16[5,2,1792,64]{2,3,1,0:T(8,128)(2,1)S(1)}, bf16[5,2,1792,64]{2,3,1,0:T(8,128)(2,1)}, u32[]{:S(2)}) copy-start(bf16[5,2,1792,64]{2,3,1,0:T(8,128)(2,1)} %param.16) | copy-start | bytes 6881284
  15.6 21.0 %all-to-all-start = ((s32[128,1,14]{2,1,0:T(1,128)}), s32[128,1,14]{2,1,0:T(1,128)S(1)}, u32[]{:S(2)}, u32[]{:S(2)}) async-start(s32[128,1,14]{2,1,0:T(1,128)} %bitcast.1), calls=%async_computation | async-start | bytes 131072 | tf_op jit(solution)/shard_map/all_to_all | solution.py:76
  36.6 21.5 %all-to-all-start.1 = ((bf16[128,14,128]{2,1,0:T(8,128)(2,1)}), bf16[128,14,128]{2,1,0:T(8,128)(2,1)S(1)}, u32[]{:S(2)}, u32[]{:S(2)}) async-start(bf16[128,14,128]{2,1,0:T(8,128)(2,1)} %reshape.248), calls=%async_computation.1 | async-start | bytes 1048576 | tf_op jit(solution)/shard_map/all_to_all | solution.py:69
  44.5 125.7 %all-reduce.2.cloned.1.call-start = ((), (), s32[]{:S(2)}) async-start(), calls=%async_computation.3 | async-start | bytes 262144 | tf_op jit(solution)/shard_map/psum | solution.py:103
  67.6 5.9 %copy-start.5 = (bf16[2,2,1792,128]{3,2,1,0:T(8,128)(2,1)S(1)}, bf16[2,2,1792,128]{3,2,1,0:T(8,128)(2,1)}, u32[]{:S(2)}) copy-start(bf16[2,2,1792,128]{3,2,1,0:T(8,128)(2,1)} %param.15) | copy-start | bytes 5505028
  71.4 13.0 %collective-permute-start.11 = (f32[64,128]{1,0:T(8,128)}, f32[64,128]{1,0:T(8,128)S(1)}, u32[]{:S(2)}, u32[]{:S(2)}) collective-permute-start(f32[64,128]{1,0:T(8,128)} %get-tuple-element.17), channel_id=1, source_target_pairs={{0,1},{1,0},{2,3},{3,2},{4,5},{5,4},{6,7},{7,6},{8,9},{9,8},{10,11... | collective-permute-start | bytes 98312 | tf_op jit(solution)/shard_map/ppermute | solution.py:14
  72.5 11.9 %collective-permute-start.14 = (f32[64,128]{1,0:T(8,128)}, f32[64,128]{1,0:T(8,128)S(1)}, u32[]{:S(2)}, u32[]{:S(2)}) collective-permute-start(f32[64,128]{1,0:T(8,128)} %get-tuple-element.16), channel_id=1, source_target_pairs={{0,1},{1,0},{2,3},{3,2},{4,5},{5,4},{6,7},{7,6},{8,9},{9,8},{10,11... | collective-permute-start | bytes 98312 | tf_op jit(solution)/shard_map/ppermute | solution.py:14
  72.5 11.9 %collective-permute-start.2 = (f32[64,128]{1,0:T(8,128)}, f32[64,128]{1,0:T(8,128)S(1)}, u32[]{:S(2)}, u32[]{:S(2)}) collective-permute-start(f32[64,128]{1,0:T(8,128)} %get-tuple-element.19), channel_id=1, source_target_pairs={{0,1},{1,0},{2,3},{3,2},{4,5},{5,4},{6,7},{7,6},{8,9},{9,8},{10,11... | collective-permute-start | bytes 98312 | tf_op jit(solution)/shard_map/ppermute | solution.py:14
  73.0 12.6 %collective-permute-start.7 = (f32[64,128]{1,0:T(8,128)S(1)}, f32[64,128]{1,0:T(8,128)}, u32[]{:S(2)}, u32[]{:S(2)}) collective-permute-start(f32[64,128]{1,0:T(8,128)S(1)} %get-tuple-element.18), channel_id=1, source_target_pairs={{0,1},{1,0},{2,3},{3,2},{4,5},{5,4},{6,7},{7,6},{8,9},{9,8},{10,11... | collective-permute-start | bytes 98312 | tf_op jit(solution)/shard_map/ppermute | solution.py:14
  73.0 115.5 %collective-permute-start.16 = (bf16[64,128]{1,0:T(8,128)(2,1)}, bf16[64,128]{1,0:T(8,128)(2,1)S(1)}, u32[]{:S(2)}, u32[]{:S(2)}) collective-permute-start(bf16[64,128]{1,0:T(8,128)(2,1)} %fusion.23), channel_id=1, source_target_pairs={{0,1},{1,0},{2,3},{3,2},{4,5},{5,4},{6,7},{7,6},{8,9},{9,8},{10,11... | collective-permute-start | bytes 49160 | tf_op jit(solution)/shard_map/ppermute | solution.py:14
  84.4 111.1 %copy-start.1 = (f32[128,1792]{1,0:T(8,128)S(1)}, f32[128,1792]{1,0:T(8,128)}, u32[]{:S(2)}) copy-start(f32[128,1792]{1,0:T(8,128)} %convolution_bitcast_fusion.2) | copy-start | bytes 2752516
  84.4 0.6 copy-start.3
  85.0 0.6 copy-start.4
  86.4 86.9 %collective-permute-start.8 = (f32[64,128]{1,0:T(8,128)S(1)}, f32[64,128]{1,0:T(8,128)S(1)}, u32[]{:S(2)}, u32[]{:S(2)}) collective-permute-start(f32[64,128]{1,0:T(8,128)S(1)} %get-tuple-element.14), channel_id=1, source_target_pairs={{0,2},{2,0},{1,3},{3,1},{4,6},{6,4},{5,7},{7,5},{8,10},{10,8},{9,1... | collective-permute-start | bytes 98312 | tf_op jit(solution)/shard_map/ppermute | solution.py:14
  86.6 84.6 %collective-permute-start.3 = (f32[64,128]{1,0:T(8,128)S(1)}, f32[64,128]{1,0:T(8,128)S(1)}, u32[]{:S(2)}, u32[]{:S(2)}) collective-permute-start(f32[64,128]{1,0:T(8,128)S(1)} %get-tuple-element.15), channel_id=1, source_target_pairs={{0,2},{2,0},{1,3},{3,1},{4,6},{6,4},{5,7},{7,5},{8,10},{10,8},{9,1... | collective-permute-start | bytes 98312 | tf_op jit(solution)/shard_map/ppermute | solution.py:14
  88.0 89.6 %collective-permute-start.12 = (f32[64,128]{1,0:T(8,128)S(1)}, f32[64,128]{1,0:T(8,128)S(1)}, u32[]{:S(2)}, u32[]{:S(2)}) collective-permute-start(f32[64,128]{1,0:T(8,128)S(1)} %get-tuple-element.13), channel_id=1, source_target_pairs={{0,2},{2,0},{1,3},{3,1},{4,6},{6,4},{5,7},{7,5},{8,10},{10,8},{9,1... | collective-permute-start | bytes 98312 | tf_op jit(solution)/shard_map/ppermute | solution.py:14
  88.1 100.4 %collective-permute-start.15 = (bf16[64,128]{1,0:T(8,128)(2,1)S(1)}, bf16[64,128]{1,0:T(8,128)(2,1)S(1)}, u32[]{:S(2)}, u32[]{:S(2)}) collective-permute-start(bf16[64,128]{1,0:T(8,128)(2,1)S(1)} %get-tuple-element.12), channel_id=1, source_target_pairs={{0,2},{2,0},{1,3},{3,1},{4,6},{6,4},{5,7},{7,5},{8,10},{10,8},{9,1... | collective-permute-start | bytes 49160 | tf_op jit(solution)/shard_map/ppermute | solution.py:14
  170.2 25.3 %copy-start.2 = (bf16[2,2,1792,128]{3,2,1,0:T(8,128)(2,1)S(1)}, bf16[2,2,1792,128]{3,2,1,0:T(8,128)(2,1)}, u32[]{:S(2)}) copy-start(bf16[2,2,1792,128]{3,2,1,0:T(8,128)(2,1)} %param.14) | copy-start | bytes 5505028
  171.2 4.3 %collective-permute-start.4 = (f32[64,128]{1,0:T(8,128)S(1)}, f32[64,128]{1,0:T(8,128)S(1)}, u32[]{:S(2)}, u32[]{:S(2)}) collective-permute-start(f32[64,128]{1,0:T(8,128)S(1)} %add.137), channel_id=1, source_target_pairs={{0,4},{4,0},{1,5},{5,1},{2,6},{6,2},{3,7},{7,3},{8,12},{12,8},{9,1... | collective-permute-start | bytes 98312 | tf_op jit(solution)/shard_map/ppermute | solution.py:14
  173.3 15.6 %collective-permute-start = (f32[2,128,128]{1,2,0:T(8,128)S(1)}, f32[2,128,128]{1,2,0:T(8,128)S(1)}, u32[]{:S(2)}, u32[]{:S(2)}) collective-permute-start(f32[2,128,128]{1,2,0:T(8,128)S(1)} %pad_maximum_fusion.5), channel_id=1, source_target_pairs={{0,32},{32,0},{64,96},{96,64},{1,33},{33,1},{65,97},{97,65},{2,34}... | collective-permute-start | bytes 393224 | tf_op jit(solution)/shard_map/ppermute | solution.py:14
  175.6 5.8 %collective-permute-start.9 = (f32[64,128]{1,0:T(8,128)S(1)}, f32[64,128]{1,0:T(8,128)S(1)}, u32[]{:S(2)}, u32[]{:S(2)}) collective-permute-start(f32[64,128]{1,0:T(8,128)S(1)} %add.141), channel_id=1, source_target_pairs={{0,4},{4,0},{1,5},{5,1},{2,6},{6,2},{3,7},{7,3},{8,12},{12,8},{9,1... | collective-permute-start | bytes 98312 | tf_op jit(solution)/shard_map/ppermute | solution.py:14
  177.6 2.8 %collective-permute-start.5 = (f32[64,128]{1,0:T(8,128)S(1)}, f32[64,128]{1,0:T(8,128)S(1)}, u32[]{:S(2)}, u32[]{:S(2)}) collective-permute-start(f32[64,128]{1,0:T(8,128)S(1)} %add.138), channel_id=1, source_target_pairs={{0,8},{8,0},{1,9},{9,1},{2,10},{10,2},{3,11},{11,3},{4,12},{12,4},... | collective-permute-start | bytes 98312 | tf_op jit(solution)/shard_map/ppermute | solution.py:14
  180.4 8.1 %collective-permute-start.13 = (bf16[64,128]{1,0:T(8,128)(2,1)S(1)}, bf16[64,128]{1,0:T(8,128)(2,1)S(1)}, u32[]{:S(2)}, u32[]{:S(2)}) collective-permute-start(bf16[64,128]{1,0:T(8,128)(2,1)S(1)} %add_convert_fusion.1), channel_id=1, source_target_pairs={{0,4},{4,0},{1,5},{5,1},{2,6},{6,2},{3,7},{7,3},{8,12},{12,8},{9,1... | collective-permute-start | bytes 49160 | tf_op jit(solution)/shard_map/ppermute | solution.py:14
  181.4 4.2 %collective-permute-start.6 = (bf16[64,128]{1,0:T(8,128)(2,1)S(1)}, bf16[64,128]{1,0:T(8,128)(2,1)S(1)}, u32[]{:S(2)}, u32[]{:S(2)}) collective-permute-start(bf16[64,128]{1,0:T(8,128)(2,1)S(1)} %add_convert_fusion.3), channel_id=1, source_target_pairs={{0,16},{16,0},{1,17},{17,1},{2,18},{18,2},{3,19},{19,3},{4,20},{20... | collective-permute-start | bytes 49160 | tf_op jit(solution)/shard_map/ppermute | solution.py:14
  185.6 2.9 %collective-permute-start.10 = (bf16[64,128]{1,0:T(8,128)(2,1)S(1)}, bf16[64,128]{1,0:T(8,128)(2,1)S(1)}, u32[]{:S(2)}, u32[]{:S(2)}) collective-permute-start(bf16[64,128]{1,0:T(8,128)(2,1)S(1)} %add_convert_fusion.2), channel_id=1, source_target_pairs={{0,8},{8,0},{1,9},{9,1},{2,10},{10,2},{3,11},{11,3},{4,12},{12,4},... | collective-permute-start | bytes 49160 | tf_op jit(solution)/shard_map/ppermute | solution.py:14
  189.8 4.3 %collective-permute-start.1 = (bf16[1,128,128]{1,2,0:T(8,128)(2,1)S(1)}, bf16[1,128,128]{1,2,0:T(8,128)(2,1)S(1)}, u32[]{:S(2)}, u32[]{:S(2)}) collective-permute-start(bf16[1,128,128]{1,2,0:T(8,128)(2,1)S(1)} %get-tuple-element.22), channel_id=1, source_target_pairs={{0,64},{64,0},{32,96},{96,32},{1,65},{65,1},{33,97},{97,33},{2,66}... | collective-permute-start | bytes 98312 | tf_op jit(solution)/shard_map/ppermute | solution.py:14
Sparse Core Ops, SparseCore 0:
  74.7 95.4 all-reduce.1
where the time goes:
time: 250 us; the launch traced here: 249 us
  waiting for transfers between devices  100 us (40%)
  local copies, waits for them, and re-layouts  41.3 us (17%)
  starting transfers between devices  36.6 us (15%)
  blocking collectives  32.4 us (13%)
  matrix products  15.6 us (6%)
  between operations  13.8 us (6%)
  other arithmetic  9.57 us (4%)
    psum x1, waiting for transfers between devices, on_device(): member_summed = lax.psum(top_part, 'member')  80.7 us
    all_to_all x1, blocking collectives, on_device(): lax.all_to_all(leaving.reshape(leaves, bucket, columns), ('group', 'membe...  32.4 us
    ppermute x17, starting transfers between devices, partner(): return lax.ppermute(block, axis, route)  17.1 us
    all_to_all x1, starting transfers between devices, on_device(): lax.all_to_all(targets.reshape(leaves, bucket), ('group', 'member'), spli...  11.5 us
    dot_general x1, matrix products, on_device(): jnp.einsum('prc,pcn->rn', diag_block, paired, preferred_element_type=jnp....  9.79 us
    ppermute x17, waiting for transfers between devices, partner(): return lax.ppermute(block, axis, route)  9.46 us
    scatter x2, local copies, waits for them, and re-layouts, on_device(): jnp.zeros((capacity, columns), mesh_vector.dtype).at[slot_ids]  8.56 us
    all_to_all x1, waiting for transfers between devices, on_device(): lax.all_to_all(outgoing.reshape(leaves, bucket, columns), ('group', 'memb...  8.04 us
  transfers between devices with their start and end apart: 20, of which 8 were waited for; matrix products, arithmetic and copies ran while one was open for 11% of the time, Pallas kernels for 0%

commit v1 on v0

v1 whole, which is shorter than its diff:
```python
import jax
import jax.numpy as jnp
from jax import lax
from jax.experimental import pallas as pl
from jax.experimental.pallas import tpu as pltpu
from jax.sharding import PartitionSpec as P

LOGICAL = pl.DeviceIdType.LOGICAL
F32 = jnp.float32
BF16 = jnp.bfloat16
LEAVES = 128
LEVELS = 7
ROWS = 1024
CAP = 1792
BUCKET = 16
WINDOWS = CAP // 128
SLOTS = LEAVES * BUCKET
WIDTH = {1: 128, 2: 128, 3: 64, 4: 64, 5: 64, 6: 64, 7: 64}
START = {1: 0, 2: 128, 3: 256, 4: 320, 5: 384, 6: 448, 7: 512}
TOTAL = 576
OWNERS = {
    1: (16, 0, 4, 8),
    2: (16, 1, 2, 8),
    3: (4, 2, 4, 16),
    4: (8, 0, 1, 8),
    5: (4, 0, 1, 16),
    6: (2, 0, 1, 32),
    7: (1, 0, 1, 64),
}


def hops(step):
    ring = (0, 1, 2, 1)
    return ring[step >> 1 & 3] + ring[step >> 3 & 3] + ring[step >> 5 & 3]


def far_first(steps):
    return sorted(steps, key=lambda step: -hops(step))


def rotated(values):
    lane = lax.broadcasted_iota(jnp.int32, values.shape, 1)
    turned = pltpu.roll(values, 64, 1)
    return jnp.where(lane < 64, -turned, turned)


def one_hot(mask):
    return jnp.where(mask, 1.0, 0.0).astype(BF16)


def body(
    ranks,
    vector,
    position,
    sizes,
    diag_hbm,
    top_left_hbm,
    top_right_hbm,
    low_left_hbm,
    low_right_hbm,
    out,
    diag,
    top_right,
    low_left,
    right_t,
    left,
    spread,
    pick_t,
    put_t,
    sent,
    arrived,
    wide,
    field,
    partial,
    result,
    coef,
    returning,
    returned,
    *rest,
):
    sums = dict(zip(range(1, 8), rest[:7]))
    got = dict(zip(range(1, 7), rest[7:13]))
    load_sem, send_sem, row_sem, part_sem, coef_sem = rest[13:]
    me = lax.axis_index("group") * 32 + lax.axis_index("member")

    loads = {
        "right": [
            pltpu.make_async_copy(top_right_hbm, top_right, load_sem.at[0]),
        ]
        + [
            pltpu.make_async_copy(
                low_right_hbm.at[level, part],
                right_t.at[pl.ds(256 + level * 64, 64), pl.ds(part * CAP, CAP)],
                load_sem.at[11 + level * 2 + part],
            )
            for level in range(5)
            for part in range(2)
        ],
        "left": [pltpu.make_async_copy(low_left_hbm, low_left, load_sem.at[2])]
        + [
            pltpu.make_async_copy(
                top_left_hbm.at[level, part],
                left.at[:, pl.ds((level * 2 + part) * 128, 128)],
                load_sem.at[3 + level * 2 + part],
            )
            for level in range(2)
            for part in range(2)
        ],
        "diag": [
            pltpu.make_async_copy(
                diag_hbm.at[part, pl.ds(half * 896, 896)],
                diag.at[part, pl.ds(half * 896, 896)],
                load_sem.at[7 + part * 2 + half],
            )
            for part in range(2)
            for half in range(2)
        ],
    }
    for name in ("right", "left", "diag"):
        for copy in loads[name]:
            copy.start()

    barrier = pltpu.get_barrier_semaphore()
    everyone = far_first(range(1, LEAVES))
    for step in everyone:
        pl.semaphore_signal(barrier, inc=1, device_id=me ^ step, device_id_type=LOGICAL)

    sub = lax.broadcasted_iota(jnp.int32, (128, 128), 0)
    lane = lax.broadcasted_iota(jnp.int32, (128, 128), 1)
    size_rows = jnp.broadcast_to(sizes[...].astype(F32), (128, 128))
    ends = jnp.sum(jnp.where(lane <= sub, size_rows, 0.0), axis=1, keepdims=True)
    ends = jnp.broadcast_to(ends, (128, 128))
    where_rows, offset_rows = [], []
    for block in range(8):
        spot = position[pl.ds(block, 1), :]
        spots = jnp.broadcast_to(spot.astype(F32), (128, 128))
        past = spots >= ends
        owner = jnp.sum(jnp.where(past, 1.0, 0.0), axis=0, keepdims=True)
        begin = jnp.max(jnp.where(past, ends, 0.0), axis=0, keepdims=True)
        window = jnp.right_shift(spot, 7) - jnp.right_shift(begin.astype(jnp.int32), 7)
        where_rows.append(owner.astype(jnp.int32) * BUCKET + window)
        offset_rows.append(jnp.bitwise_and(spot, 127))
    where_cols = jnp.concatenate(where_rows, axis=0).astype(F32).T
    offset_cols = jnp.concatenate(offset_rows, axis=0).astype(F32).T
    for block in range(8):
        rows = pl.ds(block * 128, 128)
        spread[rows, pl.ds(0, 128)] = vector[rows, :]
        spread[rows, pl.ds(128, 128)] = jnp.broadcast_to(
            offset_cols[:, block : block + 1], (128, 128)
        ).astype(BF16)

    part_sub = lax.broadcasted_iota(jnp.int32, (256, 128), 0)
    bucket_row = lax.broadcasted_iota(jnp.int32, (16, 16, 128), 1)
    bucket_lane = lax.broadcasted_iota(jnp.int32, (16, 16, 128), 2)
    for chunk in range(SLOTS // 256):
        picks = jnp.concatenate(
            [one_hot(part_sub + chunk * 256 == where_rows[block]) for block in range(8)], axis=1
        )
        both = jnp.dot(picks, spread[...], preferred_element_type=F32)
        data = both[:, :128].reshape(16, 16, 128)
        offsets = both[:, 128:].reshape(16, 16, 128)
        row = jnp.sum(
            jnp.where(bucket_row == bucket_lane, offsets, 0.0), axis=1, keepdims=True
        )
        data = jnp.where(bucket_row == 14, row, data)
        sent[pl.ds(chunk * 256, 256), :] = data.reshape(256, 128).astype(BF16)

    pl.semaphore_wait(barrier, LEAVES - 1)

    def bucket(index):
        return pl.ds(pl.multiple_of(index * BUCKET, BUCKET), BUCKET)

    for step in everyone:
        other = me ^ step
        pltpu.make_async_remote_copy(
            sent.at[bucket(other)],
            arrived.at[bucket(me)],
            send_sem.at[0],
            row_sem.at[0],
            device_id=other,
            device_id_type=LOGICAL,
        ).start()
    arrived[bucket(me), :] = sent[bucket(me), :]

    for copy in loads["right"]:
        copy.wait()

    @pl.loop(0, WINDOWS)
    def _(window):
        rows = pl.ds(pl.multiple_of(window * 128, 128), 128)
        for part in range(2):
            columns = pl.ds(pl.multiple_of(part * CAP + window * 128, 128), 128)
            for level in range(2):
                right_t[pl.ds(level * 128, 128), columns] = top_right[level, part, rows, :].T

    for copy in loads["left"]:
        copy.wait()

    @pl.loop(0, WINDOWS)
    def _(window):
        rows = pl.ds(pl.multiple_of(window * 128, 128), 128)
        for level in range(5):
            left[rows, pl.ds(512 + level * 128, 128)] = low_left[level, :, rows].T

    for block in range(8):
        column = jnp.broadcast_to(where_cols[:, block : block + 1], (128, 128)).astype(jnp.int32)
        for piece in range(SLOTS // 128):
            pick_t[pl.ds(block * 128, 128), pl.ds(piece * 128, 128)] = one_hot(
                column == lane + piece * 128
            )

    def landed(buffer, rows, semaphore):
        view = buffer.at[pl.ds(0, rows)]
        pltpu.make_async_copy(view, view, semaphore).wait()

    landed(arrived, SLOTS - BUCKET, row_sem.at[0])

    wide[...] = arrived[...].astype(F32)
    offsets = wide[pl.ds(14, 128, stride=16), :]
    offsets_t = offsets.T
    sub_f = sub.astype(F32)
    lane_f = lane.astype(F32)
    for window in range(WINDOWS):
        put = one_hot(jnp.broadcast_to(offsets_t[window : window + 1, :], (128, 128)) == sub_f)
        rows = wide[pl.ds(window, 128, stride=16), :].astype(BF16)
        values = jnp.dot(put, rows, preferred_element_type=F32)
        field[pl.ds(window * 128, 128), :] = values.astype(BF16)
        field[pl.ds(CAP + window * 128, 128), :] = rotated(values).astype(BF16)

    for level in range(1, 8):
        count, first, apart, rows = OWNERS[level]
        members = 1 << (LEVELS - level)
        begin, width = START[level], WIDTH[level]
        partial[pl.ds(begin, width), :] = jnp.dot(
            right_t[pl.ds(begin, width), :], field[...], preferred_element_type=F32
        )
        node = ((me >> (LEVELS - level)) ^ 1) << (LEVELS - level)
        place = me & (members - 1)
        for step in far_first(range(count)):
            index = (place // apart) ^ step
            pltpu.make_async_remote_copy(
                partial.at[pl.ds(pl.multiple_of(begin + index * rows, 8), rows)],
                sums[level].at[pl.ds(pl.multiple_of(place * rows, 8), rows)],
                send_sem.at[1],
                part_sem.at[level - 1],
                device_id=node + first + index * apart,
                device_id_type=LOGICAL,
            ).start()

    for copy in loads["diag"]:
        copy.wait()

    @pl.loop(0, CAP // 256)
    def _(chunk):
        rows = pl.ds(pl.multiple_of(chunk * 256, 256), 256)
        result[rows, :] = jnp.dot(
            diag[0, rows, :], field[pl.ds(0, CAP), :], preferred_element_type=F32
        ) + jnp.dot(diag[1, rows, :], field[pl.ds(CAP, CAP), :], preferred_element_type=F32)

    for window in range(WINDOWS):
        column = jnp.broadcast_to(offsets[:, window : window + 1], (128, 128))
        put_t[pl.ds(window * 128, 128), :] = one_hot(column == lane_f)

    for level in range(1, 7):
        count, first, apart, rows = OWNERS[level]
        members = 1 << (LEVELS - level)
        place = me & (members - 1)
        index = place // apart

        @pl.when(place % apart == first)
        def _(level=level, rows=rows, members=members, index=index):
            landed(sums[level], members * rows, part_sem.at[level - 1])
            total = jnp.sum(sums[level][...].reshape(members, rows, 128), axis=0)
            rank = ranks[(1 << level) - 2 + (me >> (LEVELS - level))]
            row = lax.broadcasted_iota(jnp.int32, (rows, 128), 0) + index * rows
            mine = pl.ds(pl.multiple_of(index * rows, 8), rows)
            got[level][mine, :] = jnp.where(row < rank, total, 0.0)
            for step in far_first(range(1, members)):
                pltpu.make_async_remote_copy(
                    got[level].at[mine],
                    got[level].at[mine],
                    send_sem.at[2],
                    coef_sem.at[level - 1],
                    device_id=me ^ step,
                    device_id_type=LOGICAL,
                ).start()

    def set_coef(level, values):
        begin = START[level] * 2
        width = WIDTH[level]
        values = values.astype(BF16).astype(F32)
        coef[pl.ds(begin, width), :] = values.astype(BF16)
        coef[pl.ds(begin + width, width), :] = rotated(values).astype(BF16)

    landed(sums[7], 64, part_sem.at[6])
    row = lax.broadcasted_iota(jnp.int32, (64, 128), 0)
    set_coef(7, jnp.where(row < ranks[(1 << 7) - 2 + me], sums[7][...], 0.0))
    for level in range(6, 0, -1):
        count, first, apart, rows = OWNERS[level]
        members = 1 << (LEVELS - level)
        owner = (me & (members - 1)) % apart == first

        @pl.when(owner)
        def _(level=level, rows=rows):
            landed(got[level], WIDTH[level] - rows, coef_sem.at[level - 1])

        if apart > 1:

            @pl.when(jnp.logical_not(owner))
            def _(level=level):
                landed(got[level], WIDTH[level], coef_sem.at[level - 1])

        set_coef(level, got[level][...])

    wide[pl.ds(14, 128, stride=16), :] = jnp.zeros((128, 128), F32)
    wide[pl.ds(15, 128, stride=16), :] = jnp.zeros((128, 128), F32)
    for chunk in range(CAP // 256):
        rows = pl.ds(chunk * 256, 256)
        values = result[rows, :] + jnp.dot(left[rows, :], coef[...], preferred_element_type=F32)
        values = values.astype(BF16)
        for half in range(2):
            window = chunk * 2 + half
            wide[pl.ds(window, 128, stride=16), :] = jnp.dot(
                put_t[pl.ds(window * 128, 128), :],
                values[half * 128 : half * 128 + 128],
                preferred_element_type=F32,
            )
    returning[...] = wide[...].astype(BF16)
    for step in everyone:
        other = me ^ step
        pltpu.make_async_remote_copy(
            returning.at[bucket(other)],
            returned.at[bucket(me)],
            send_sem.at[3],
            row_sem.at[1],
            device_id=other,
            device_id_type=LOGICAL,
        ).start()
    returned[bucket(me), :] = returning[bucket(me), :]

    landed(sent, SLOTS - BUCKET, send_sem.at[0])
    landed(partial, TOTAL, send_sem.at[1])
    for level in range(1, 7):
        count, first, apart, rows = OWNERS[level]
        members = 1 << (LEVELS - level)

        @pl.when((me & (members - 1)) % apart == first)
        def _(level=level, rows=rows, members=members):
            landed(sums[level], (members - 1) * rows, send_sem.at[2])

    landed(returned, SLOTS - BUCKET, row_sem.at[1])

    @pl.loop(0, ROWS // 256)
    def _(chunk):
        rows = pl.ds(pl.multiple_of(chunk * 256, 256), 256)
        out[rows, :] = jnp.dot(pick_t[rows, :], returned[...], preferred_element_type=F32)

    landed(returning, SLOTS - BUCKET, send_sem.at[3])


def on_device(
    mesh_vector,
    cluster_position,
    cluster_sizes,
    block_ranks,
    diag_block,
    top_left,
    top_right,
    low_left,
    low_right,
):
    vmem = pl.BlockSpec(memory_space=pltpu.VMEM)
    anywhere = pl.BlockSpec(memory_space=pl.ANY)
    scratch = [
        pltpu.VMEM((2, CAP, CAP), BF16),
        pltpu.VMEM((2, 2, CAP, 128), BF16),
        pltpu.VMEM((5, 128, CAP), BF16),
        pltpu.VMEM((TOTAL, 2 * CAP), BF16),
        pltpu.VMEM((CAP, 2 * TOTAL), BF16),
        pltpu.VMEM((ROWS, 256), BF16),
        pltpu.VMEM((ROWS, SLOTS), BF16),
        pltpu.VMEM((CAP, 128), BF16),
        pltpu.VMEM((SLOTS, 128), BF16),
        pltpu.VMEM((SLOTS, 128), BF16),
        pltpu.VMEM((SLOTS, 128), F32),
        pltpu.VMEM((2 * CAP, 128), BF16),
        pltpu.VMEM((TOTAL, 128), F32),
        pltpu.VMEM((CAP, 128), F32),
        pltpu.VMEM((2 * TOTAL, 128), BF16),
        pltpu.VMEM((SLOTS, 128), BF16),
        pltpu.VMEM((SLOTS, 128), BF16),
    ]
    scratch += [
        pltpu.VMEM(((1 << (LEVELS - level)) * OWNERS[level][3], 128), F32) for level in range(1, 8)
    ]
    scratch += [pltpu.VMEM((WIDTH[level], 128), F32) for level in range(1, 7)]
    scratch += [
        pltpu.SemaphoreType.DMA((21,)),
        pltpu.SemaphoreType.DMA((4,)),
        pltpu.SemaphoreType.DMA((2,)),
        pltpu.SemaphoreType.DMA((7,)),
        pltpu.SemaphoreType.DMA((6,)),
    ]
    return pl.pallas_call(
        body,
        out_shape=jax.ShapeDtypeStruct((ROWS, 128), F32),
        in_specs=[pl.BlockSpec(memory_space=pltpu.SMEM), vmem, vmem, vmem] + [anywhere] * 5,
        out_specs=vmem,
        scratch_shapes=scratch,
        compiler_params=pltpu.CompilerParams(
            collective_id=0, has_side_effects=True, vmem_limit_bytes=56 * 2**20
        ),
        name="tree_product",
    )(
        block_ranks,
        mesh_vector,
        cluster_position.reshape(8, 128),
        cluster_sizes.reshape(1, 128),
        diag_block,
        top_left,
        top_right,
        jnp.swapaxes(low_left, 2, 3).reshape(5, 128, CAP),
        jnp.swapaxes(low_right, 2, 3),
    )


def solution(mesh):
    return jax.shard_map(
        on_device,
        mesh=mesh,
        in_specs=(
            P(("group", "member"), None),
            P(("group", "member")),
            P(),
            P(),
            P(None, ("group", "member"), None),
            P(None, None, ("group", "member"), None),
            P(None, None, ("group", "member"), None),
            P(None, None, ("group", "member"), None),
            P(None, None, ("group", "member"), None),
        ),
        out_specs=P(("group", "member"), None),
        check_vma=False,
    )
```

time: 250 us -> 49.9 us (0.20)
  waiting for transfers between devices: 100 us -> 0 us
  Pallas kernels: 0 us -> 47.9 us
  local copies, waits for them, and re-layouts: 41.3 us -> 1.87 us
  starting transfers between devices: 36.6 us -> 0 us
  blocking collectives: 32.4 us -> 0 us
  matrix products: 15.6 us -> 0 us
  between operations: 13.8 us -> 0.01 us
  other arithmetic: 9.57 us -> 0 us
    psum x1 -> x0, waiting for transfers between devices: 80.7 us -> none  [on_device(): member_summed = lax.psum(top_part, 'member')]
    pallas_call x0 -> x1, Pallas kernels: none -> 47.9 us  [on_device(): pl.pallas_call(body, out_shape=jax.ShapeDtypeStruct((ROWS, 128), F32), in...]
    all_to_all x1 -> x0, blocking collectives: 32.4 us -> none  [on_device(): lax.all_to_all(leaving.reshape(leaves, bucket, columns), ('group', 'membe...]
    all_to_all x2 -> x0, starting transfers between devices: 19.4 us -> none  [the longest x1 11.5 us: on_device(): lax.all_to_all(targets.reshape(leaves, bucket), ('group', 'member'), spli...]
    ppermute x17 -> x0, starting transfers between devices: 17.1 us -> none  [partner(): return lax.ppermute(block, axis, route)]
    scatter x4 -> x0, local copies, waits for them, and re-layouts: 16.5 us -> none  [the longest x2 8.56 us: on_device(): jnp.zeros((capacity, columns), mesh_vector.dtype).at[slot_ids]]
    dot_general x5 -> x0, matrix products: 15.6 us -> none  [the longest x1 9.79 us: on_device(): jnp.einsum('prc,pcn->rn', diag_block, paired, preferred_element_type=jnp....]
    all_to_all x2 -> x0, waiting for transfers between devices: 9.87 us -> none  [the longest x1 8.04 us: on_device(): lax.all_to_all(outgoing.reshape(leaves, bucket, columns), ('group', 'memb...]
  transfers between devices with their start and end apart: 20 -> 0, of which waited for: 8 -> 0; matrix products, arithmetic and copies ran while one was open for 11% -> 0% of each run, Pallas kernels for 0% -> 0%
where the time goes in v1:
time: 49.9 us; the launch traced here: 49.7 us
  Pallas kernels  47.9 us (96%)
  local copies, waits for them, and re-layouts  1.87 us (4%)
    pallas_call x1, Pallas kernels, on_device(): pl.pallas_call(body, out_shape=jax.ShapeDtypeStruct((ROWS, 128), F32), in...  47.9 us
    unnamed x1, local copies, waits for them, and re-layouts  1.87 us

profile of v1, /device:TPU:1, one launch (start us, length us, event | category | flops | bytes accessed | tf_op | source)
XLA Modules:
  0.0 49.7 jit_solution(17903109225172493263)
XLA Ops:
  0.0 47.9 %tree_product.1 = f32[1024,128]{1,0:T(8,128)} custom-call(s32[254]{0:T(256)} %ranks.1, bf16[1024,128]{1,0:T(8,128)(2,1)} %vector.1, s32[8,128]{1,0:T(8,128)} %bitcast.8, s32[1,128]{1,0:T(1,128)} %bitcast.9, bf16[2,1792,1792]{2,1,0:T(8,128)(2,1)} %diag_hbm.1, bf16[2,2,1792,128]{3,2,1,0:T(8,128)(2,1)} %top_left_hbm.1, bf16[2,2,1792,128]{3,2,1,0:T(8,128)(2,1)} %top_right_hbm.1, ...), custom_call_target="tpu_custom_call" | custom-call | tf_op jit(solution)/shard_map/tree_product/pallas_call | solution.py:404
  47.9 1.9 %copy.11 = f32[1024,128]{1,0:T(8,128)} copy(f32[1024,128]{1,0:T(8,128)} %tree_product.1) | data formatting | bytes 1048576

commit v2 on v1

--- a/solution.py
+++ b/solution.py
@@ -18,11 +18,12 @@
 WIDTH = {1: 128, 2: 128, 3: 64, 4: 64, 5: 64, 6: 64, 7: 64}
 START = {1: 0, 2: 128, 3: 256, 4: 320, 5: 384, 6: 448, 7: 512}
 TOTAL = 576
+TURNS = (0, 32, 64, 96, 128)
 OWNERS = {
-    1: (16, 0, 4, 8),
-    2: (16, 1, 2, 8),
+    1: (8, 0, 4, 16),
+    2: (8, 1, 4, 16),
     3: (4, 2, 4, 16),
-    4: (8, 0, 1, 8),
+    4: (4, 1, 2, 16),
     5: (4, 0, 1, 16),
     6: (2, 0, 1, 32),
     7: (1, 0, 1, 64),
@@ -38,6 +39,18 @@
     return sorted(steps, key=lambda step: -hops(step))
 
 
+def sources_of(level):
+    return 1 << (LEVELS - level)
+
+
+def region_of(level):
+    return min(sources_of(level), 32)
+
+
+def turn_of(place):
+    return sum(place >= begin for begin in TURNS[1:-1])
+
+
 def rotated(values):
     lane = lax.broadcasted_iota(jnp.int32, values.shape, 1)
     turned = pltpu.roll(values, 64, 1)
@@ -49,16 +62,20 @@
 
 
 def body(
-    ranks,
-    vector,
-    position,
-    sizes,
+    ranks_hbm,
+    vector_hbm,
+    position_hbm,
+    sizes_hbm,
     diag_hbm,
     top_left_hbm,
     top_right_hbm,
     low_left_hbm,
     low_right_hbm,
-    out,
+    product,
+    ranks,
+    vector,
+    position,
+    sizes,
     diag,
     top_right,
     low_left,
@@ -82,6 +99,24 @@
     got = dict(zip(range(1, 7), rest[7:13]))
     load_sem, send_sem, row_sem, part_sem, coef_sem = rest[13:]
     me = lax.axis_index("group") * 32 + lax.axis_index("member")
+
+    first_loads = [
+        pltpu.make_async_copy(source, target, load_sem.at[21 + index])
+        for index, (source, target) in enumerate(
+            (
+                (position_hbm, position),
+                (sizes_hbm, sizes),
+                (vector_hbm, vector),
+                (ranks_hbm, ranks),
+            )
+        )
+    ]
+    for copy in first_loads:
+        copy.start()
+    barrier = pltpu.get_barrier_semaphore()
+    everyone = far_first(range(1, LEAVES))
+    for step in everyone:
+        pl.semaphore_signal(barrier, inc=1, device_id=me ^ step, device_id_type=LOGICAL)
 
     loads = {
         "right": [
@@ -119,18 +154,15 @@
     for name in ("right", "left", "diag"):
         for copy in loads[name]:
             copy.start()
-
-    barrier = pltpu.get_barrier_semaphore()
-    everyone = far_first(range(1, LEAVES))
-    for step in everyone:
-        pl.semaphore_signal(barrier, inc=1, device_id=me ^ step, device_id_type=LOGICAL)
+    for copy in first_loads:
+        copy.wait()
 
     sub = lax.broadcasted_iota(jnp.int32, (128, 128), 0)
     lane = lax.broadcasted_iota(jnp.int32, (128, 128), 1)
     size_rows = jnp.broadcast_to(sizes[...].astype(F32), (128, 128))
     ends = jnp.sum(jnp.where(lane <= sub, size_rows, 0.0), axis=1, keepdims=True)
     ends = jnp.broadcast_to(ends, (128, 128))
-    where_rows, offset_rows = [], []
+    where_rows, window_rows, owner_rows, offset_rows = [], [], [], []
     for block in range(8):
         spot = position[pl.ds(block, 1), :]
         spots = jnp.broadcast_to(spot.astype(F32), (128, 128))
@@ -138,9 +170,10 @@
         owner = jnp.sum(jnp.where(past, 1.0, 0.0), axis=0, keepdims=True)
         begin = jnp.max(jnp.where(past, ends, 0.0), axis=0, keepdims=True)
         window = jnp.right_shift(spot, 7) - jnp.right_shift(begin.astype(jnp.int32), 7)
+        owner_rows.append(owner)
+        window_rows.append(window)
         where_rows.append(owner.astype(jnp.int32) * BUCKET + window)
         offset_rows.append(jnp.bitwise_and(spot, 127))
-    where_cols = jnp.concatenate(where_rows, axis=0).astype(F32).T
     offset_cols = jnp.concatenate(offset_rows, axis=0).astype(F32).T
     for block in range(8):
         rows = pl.ds(block * 128, 128)
@@ -202,8 +235,19 @@
         for level in range(5):
             left[rows, pl.ds(512 + level * 128, 128)] = low_left[level, :, rows].T
 
+    steps = jnp.bitwise_xor(lax.broadcasted_iota(jnp.int32, (1, 128), 1), me)
+    places = jnp.full((1, 128), LEAVES - 1, jnp.int32)
+    for place, step in enumerate(everyone):
+        places = jnp.where(steps == step, place, places)
+    places = jnp.broadcast_to(places.astype(F32), (128, 128)).T
+    where_back = []
     for block in range(8):
-        column = jnp.broadcast_to(where_cols[:, block : block + 1], (128, 128)).astype(jnp.int32)
+        owners = jnp.broadcast_to(owner_rows[block], (128, 128)).astype(jnp.int32)
+        place = jnp.sum(jnp.where(owners == sub, places, 0.0), axis=0, keepdims=True)
+        where_back.append(place * BUCKET + window_rows[block].astype(F32))
+    where_back = jnp.concatenate(where_back, axis=0).T
+    for block in range(8):
+        column = jnp.broadcast_to(where_back[:, block : block + 1], (128, 128)).astype(jnp.int32)
         for piece in range(SLOTS // 128):
             pick_t[pl.ds(block * 128, 128), pl.ds(piece * 128, 128)] = one_hot(
                 column == lane + piece * 128
@@ -227,25 +271,25 @@
         field[pl.ds(window * 128, 128), :] = values.astype(BF16)
         field[pl.ds(CAP + window * 128, 128), :] = rotated(values).astype(BF16)
 
-    for level in range(1, 8):
-        count, first, apart, rows = OWNERS[level]
-        members = 1 << (LEVELS - level)
-        begin, width = START[level], WIDTH[level]
-        partial[pl.ds(begin, width), :] = jnp.dot(
-            right_t[pl.ds(begin, width), :], field[...], preferred_element_type=F32
-        )
-        node = ((me >> (LEVELS - level)) ^ 1) << (LEVELS - level)
-        place = me & (members - 1)
-        for step in far_first(range(count)):
-            index = (place // apart) ^ step
-            pltpu.make_async_remote_copy(
-                partial.at[pl.ds(pl.multiple_of(begin + index * rows, 8), rows)],
-                sums[level].at[pl.ds(pl.multiple_of(place * rows, 8), rows)],
-                send_sem.at[1],
-                part_sem.at[level - 1],
-                device_id=node + first + index * apart,
-                device_id_type=LOGICAL,
-            ).start()
+    for levels in ((1, 2), (3, 4, 5, 6, 7)):
+        span = pl.ds(START[levels[0]], sum(WIDTH[level] for level in levels))
+        partial[span, :] = jnp.dot(right_t[span, :], field[...], preferred_element_type=F32)
+        for level in levels:
+            count, first, apart, rows = OWNERS[level]
+            node = ((me >> (LEVELS - level)) ^ 1) << (LEVELS - level)
+            place = me & (sources_of(level) - 1)
+            index = (place & (region_of(level) - 1)) // apart
+            for group in range(sources_of(level) // region_of(level)):
+                for step in far_first(range(count)):
+                    piece = index ^ step
+                    pltpu.make_async_remote_copy(
+                        partial.at[pl.ds(pl.multiple_of(START[level] + piece * rows, 8), rows)],
+                        sums[level].at[pl.ds(pl.multiple_of(place * rows, 8), rows)],
+                        send_sem.at[1],
+                        part_sem.at[level - 1],
+                        device_id=node + group * 32 + first + piece * apart,
+                        device_id_type=LOGICAL,
+                    ).start()
 
     for copy in loads["diag"]:
         copy.wait()
@@ -259,23 +303,26 @@
 
     for window in range(WINDOWS):
         column = jnp.broadcast_to(offsets[:, window : window + 1], (128, 128))
-        put_t[pl.ds(window * 128, 128), :] = one_hot(column == lane_f)
-
-    for level in range(1, 7):
+        rows = pl.ds(window * 128, 128)
+        put_t[rows, pl.ds(window % 2 * 128, 128)] = one_hot(column == lane_f)
+        put_t[rows, pl.ds(128 - window % 2 * 128, 128)] = jnp.zeros((128, 128), BF16)
+    wide[pl.ds(14, 128, stride=16), :] = jnp.zeros((128, 128), F32)
+    wide[pl.ds(15, 128, stride=16), :] = jnp.zeros((128, 128), F32)
+
+    for level in range(6, 0, -1):
         count, first, apart, rows = OWNERS[level]
-        members = 1 << (LEVELS - level)
-        place = me & (members - 1)
-        index = place // apart
+        place = me & (region_of(level) - 1)
 
         @pl.when(place % apart == first)
-        def _(level=level, rows=rows, members=members, index=index):
-            landed(sums[level], members * rows, part_sem.at[level - 1])
-            total = jnp.sum(sums[level][...].reshape(members, rows, 128), axis=0)
+        def _(level=level, rows=rows, index=place // apart):
+            sources = sources_of(level)
+            landed(sums[level], sources * rows, part_sem.at[level - 1])
+            total = jnp.sum(sums[level][...].reshape(sources, rows, 128), axis=0)
             rank = ranks[(1 << level) - 2 + (me >> (LEVELS - level))]
             row = lax.broadcasted_iota(jnp.int32, (rows, 128), 0) + index * rows
-            mine = pl.ds(pl.multiple_of(index * rows, 8), rows)
-            got[level][mine, :] = jnp.where(row < rank, total, 0.0)
-            for step in far_first(range(1, members)):
+            mine = pl.ds(pl.multiple_of(index * rows, 16), rows)
+            got[level][mine, :] = jnp.where(row < rank, total, 0.0).astype(BF16)
+            for step in far_first(range(1, region_of(level))):
                 pltpu.make_async_remote_copy(
                     got[level].at[mine],
                     got[level].at[mine],
@@ -288,73 +335,86 @@
     def set_coef(level, values):
         begin = START[level] * 2
         width = WIDTH[level]
-        values = values.astype(BF16).astype(F32)
-        coef[pl.ds(begin, width), :] = values.astype(BF16)
-        coef[pl.ds(begin + width, width), :] = rotated(values).astype(BF16)
+        coef[pl.ds(begin, width), :] = values
+        coef[pl.ds(begin + width, width), :] = rotated(values.astype(F32)).astype(BF16)
 
     landed(sums[7], 64, part_sem.at[6])
     row = lax.broadcasted_iota(jnp.int32, (64, 128), 0)
-    set_coef(7, jnp.where(row < ranks[(1 << 7) - 2 + me], sums[7][...], 0.0))
-    for level in range(6, 0, -1):
+    set_coef(7, jnp.where(row < ranks[(1 << 7) - 2 + me], sums[7][...], 0.0).astype(BF16))
+
+    def await_coef(level):
         count, first, apart, rows = OWNERS[level]
-        members = 1 << (LEVELS - level)
-        owner = (me & (members - 1)) % apart == first
+        owner = (me & (region_of(level) - 1)) % apart == first
 
         @pl.when(owner)
-        def _(level=level, rows=rows):
+        def _():
             landed(got[level], WIDTH[level] - rows, coef_sem.at[level - 1])
 
         if apart > 1:
 
             @pl.when(jnp.logical_not(owner))
-            def _(level=level):
+            def _():
                 landed(got[level], WIDTH[level], coef_sem.at[level - 1])
 
         set_coef(level, got[level][...])
 
-    wide[pl.ds(14, 128, stride=16), :] = jnp.zeros((128, 128), F32)
-    wide[pl.ds(15, 128, stride=16), :] = jnp.zeros((128, 128), F32)
+    for level in range(6, 2, -1):
+        await_coef(level)
     for chunk in range(CAP // 256):
         rows = pl.ds(chunk * 256, 256)
-        values = result[rows, :] + jnp.dot(left[rows, :], coef[...], preferred_element_type=F32)
-        values = values.astype(BF16)
+        result[rows, :] += jnp.dot(
+            left[rows, pl.ds(512, 640)], coef[pl.ds(512, 640), :], preferred_element_type=F32
+        )
+    for level in (2, 1):
+        await_coef(level)
+
+    for chunk in range(CAP // 256):
+        rows = pl.ds(chunk * 256, 256)
+        values = result[rows, :] + jnp.dot(
+            left[rows, pl.ds(0, 512)], coef[pl.ds(0, 512), :], preferred_element_type=F32
+        )
+        field[rows, :] = values.astype(BF16)
+    for chunk in range(CAP // 256):
+        rows = pl.ds(chunk * 256, 256)
+        leaving = jnp.dot(put_t[rows, :], field[rows, :], preferred_element_type=F32)
         for half in range(2):
-            window = chunk * 2 + half
-            wide[pl.ds(window, 128, stride=16), :] = jnp.dot(
-                put_t[pl.ds(window * 128, 128), :],
-                values[half * 128 : half * 128 + 128],
-                preferred_element_type=F32,
-            )
+            wide[pl.ds(chunk * 2 + half, 128, stride=16), :] = leaving[half * 128 : half * 128 + 128]
     returning[...] = wide[...].astype(BF16)
-    for step in everyone:
+    for place, step in enumerate(everyone):
         other = me ^ step
         pltpu.make_async_remote_copy(
             returning.at[bucket(other)],
-            returned.at[bucket(me)],
+            returned.at[pl.ds(place * BUCKET, BUCKET)],
             send_sem.at[3],
-            row_sem.at[1],
+            row_sem.at[1 + turn_of(place)],
             device_id=other,
             device_id_type=LOGICAL,
         ).start()
-    returned[bucket(me), :] = returning[bucket(me), :]
+    returned[pl.ds(SLOTS - BUCKET, BUCKET), :] = returning[bucket(me), :]
 
     landed(sent, SLOTS - BUCKET, send_sem.at[0])
     landed(partial, TOTAL, send_sem.at[1])
+    landed(partial, WIDTH[1], send_sem.at[1])
     for level in range(1, 7):
         count, first, apart, rows = OWNERS[level]
-        members = 1 << (LEVELS - level)
-
-        @pl.when((me & (members - 1)) % apart == first)
-        def _(level=level, rows=rows, members=members):
-            landed(sums[level], (members - 1) * rows, send_sem.at[2])
-
-    landed(returned, SLOTS - BUCKET, row_sem.at[1])
-
-    @pl.loop(0, ROWS // 256)
-    def _(chunk):
-        rows = pl.ds(pl.multiple_of(chunk * 256, 256), 256)
-        out[rows, :] = jnp.dot(pick_t[rows, :], returned[...], preferred_element_type=F32)
-
+
+        @pl.when((me & (region_of(level) - 1)) % apart == first)
+        def _(level=level, rows=rows):
+            landed(sent, (region_of(level) - 1) * rows, send_sem.at[2])
+
+    for turn, (begin, end) in enumerate(zip(TURNS[:-1], TURNS[1:])):
+        count = (end - begin) * BUCKET
+        landed(returned, count - BUCKET if end == LEAVES else count, row_sem.at[1 + turn])
+        span = pl.ds(begin * BUCKET, count)
+        for chunk in range(ROWS // 256):
+            rows = pl.ds(chunk * 256, 256)
+            total = jnp.dot(pick_t[rows, span], returned[span, :], preferred_element_type=F32)
+            if turn > 0:
+                total += result[rows, :]
+            if end < LEAVES:
+                result[rows, :] = total
+            else:
+                product[rows, :] = total.astype(BF16)
     landed(returning, SLOTS - BUCKET, send_sem.at[3])
 
 
@@ -369,9 +429,11 @@
     low_left,
     low_right,
 ):
-    vmem = pl.BlockSpec(memory_space=pltpu.VMEM)
-    anywhere = pl.BlockSpec(memory_space=pl.ANY)
     scratch = [
+        pltpu.SMEM((254,), jnp.int32),
+        pltpu.VMEM((ROWS, 128), BF16),
+        pltpu.VMEM((8, 128), jnp.int32),
+        pltpu.VMEM((1, 128), jnp.int32),
         pltpu.VMEM((2, CAP, CAP), BF16),
         pltpu.VMEM((2, 2, CAP, 128), BF16),
         pltpu.VMEM((5, 128, CAP), BF16),
@@ -379,7 +441,7 @@
         pltpu.VMEM((CAP, 2 * TOTAL), BF16),
         pltpu.VMEM((ROWS, 256), BF16),
         pltpu.VMEM((ROWS, SLOTS), BF16),
-        pltpu.VMEM((CAP, 128), BF16),
+        pltpu.VMEM((CAP, 256), BF16),
         pltpu.VMEM((SLOTS, 128), BF16),
         pltpu.VMEM((SLOTS, 128), BF16),
         pltpu.VMEM((SLOTS, 128), F32),
@@ -393,25 +455,25 @@
     scratch += [
         pltpu.VMEM(((1 << (LEVELS - level)) * OWNERS[level][3], 128), F32) for level in range(1, 8)
     ]
-    scratch += [pltpu.VMEM((WIDTH[level], 128), F32) for level in range(1, 7)]
+    scratch += [pltpu.VMEM((WIDTH[level], 128), BF16) for level in range(1, 7)]
     scratch += [
-        pltpu.SemaphoreType.DMA((21,)),
+        pltpu.SemaphoreType.DMA((25,)),
         pltpu.SemaphoreType.DMA((4,)),
-        pltpu.SemaphoreType.DMA((2,)),
+        pltpu.SemaphoreType.DMA((5,)),
         pltpu.SemaphoreType.DMA((7,)),
         pltpu.SemaphoreType.DMA((6,)),
     ]
-    return pl.pallas_call(
+    product = pl.pallas_call(
         body,
-        out_shape=jax.ShapeDtypeStruct((ROWS, 128), F32),
-        in_specs=[pl.BlockSpec(memory_space=pltpu.SMEM), vmem, vmem, vmem] + [anywhere] * 5,
-        out_specs=vmem,
+        out_shape=pltpu.VMEM((ROWS, 128), BF16),
+        in_specs=[pl.BlockSpec(memory_space=pltpu.HBM)] * 9,
+        out_specs=pl.BlockSpec(memory_space=pltpu.VMEM),
         scratch_shapes=scratch,
         compiler_params=pltpu.CompilerParams(
-            collective_id=0, has_side_effects=True, vmem_limit_bytes=56 * 2**20
+            collective_id=0, has_side_effects=True, vmem_limit_bytes=53 * 2**20
         ),
         name="tree_product",
-    )(
+    )(*(pltpu.with_memory_space_constraint(operand, pltpu.HBM) for operand in (
         block_ranks,
         mesh_vector,
         cluster_position.reshape(8, 128),
@@ -421,7 +483,8 @@
         top_right,
         jnp.swapaxes(low_left, 2, 3).reshape(5, 128, CAP),
         jnp.swapaxes(low_right, 2, 3),
-    )
+    )))
+    return product.astype(F32)
 
 
 def solution(mesh):

time: 49.9 us -> 46.2 us (0.926)
  Pallas kernels: 47.9 us -> 45.3 us
  local copies, waits for them, and re-layouts: 1.87 us -> 0 us
  other arithmetic: 0 us -> 0.83 us
    pallas_call x1, Pallas kernels: 47.9 us -> 45.3 us  [on_device(): pl.pallas_call(body, out_shape=pltpu.VMEM((ROWS, 128), BF16), in_specs=[p...]
    unnamed x1 -> x0, local copies, waits for them, and re-layouts: 1.87 us -> none
    convert_element_type x0 -> x1, other arithmetic: none -> 0.83 us  [on_device(): return product.astype(F32)]
where the time goes in v2:
time: 46.2 us; the launch traced here: 46.1 us
  Pallas kernels  45.3 us (98%)
  other arithmetic  0.83 us (2%)
    pallas_call x1, Pallas kernels, on_device(): pl.pallas_call(body, out_shape=pltpu.VMEM((ROWS, 128), BF16), in_specs=[p...  45.3 us

profile of v2, /device:TPU:1, one launch (start us, length us, event | category | flops | bytes accessed | tf_op | source)
XLA Modules:
  0.0 46.1 jit_solution(8905149329346956497)
XLA Ops:
  0.0 45.3 %tree_product.1 = bf16[1024,128]{1,0:T(8,128)(2,1)S(1)} custom-call(s32[254]{0:T(256)} %ranks_hbm.1, bf16[1024,128]{1,0:T(8,128)(2,1)} %vector_hbm.1, s32[8,128]{1,0:T(8,128)} %bitcast.8, s32[1,128]{1,0:T(1,128)} %bitcast.9, bf16[2,1792,1792]{2,1,0:T(8,128)(2,1)} %diag_hbm.1, bf16[2,2,1792,128]{3,2,1,0:T(8,128)(2,1)} %top_left_hbm.1, ...), custom_call_target="tpu_custom_call" | custom-call | tf_op jit(solution)/shard_map/tree_product/pallas_call | solution.py:466
  45.3 0.8 %convert_element_type.3 = f32[1024,128]{1,0:T(8,128)} convert(bf16[1024,128]{1,0:T(8,128)(2,1)S(1)} %tree_product.1) | non-fusion elementwise | flops 131072 | bytes 786432 | tf_op jit(solution)/shard_map/convert_element_type | solution.py:487

commit v3 on v2

--- a/solution.py
+++ b/solution.py
@@ -20,9 +20,9 @@
 TOTAL = 576
 TURNS = (0, 32, 64, 96, 128)
 OWNERS = {
-    1: (8, 0, 4, 16),
-    2: (8, 1, 4, 16),
-    3: (4, 2, 4, 16),
+    1: (16, 0, 4, 8),
+    2: (8, 3, 4, 16),
+    3: (4, 1, 4, 16),
     4: (4, 1, 2, 16),
     5: (4, 0, 1, 16),
     6: (2, 0, 1, 32),
@@ -36,15 +36,15 @@
 
 
 def far_first(steps):
-    return sorted(steps, key=lambda step: -hops(step))
+    return sorted(steps, key=lambda step: (-hops(step), -(step & 1)))
 
 
 def sources_of(level):
     return 1 << (LEVELS - level)
 
 
-def region_of(level):
-    return min(sources_of(level), 32)
+def sum_type(level):
+    return BF16 if OWNERS[level][3] >= 16 else F32
 
 
 def turn_of(place):
@@ -278,18 +278,17 @@
             count, first, apart, rows = OWNERS[level]
             node = ((me >> (LEVELS - level)) ^ 1) << (LEVELS - level)
             place = me & (sources_of(level) - 1)
-            index = (place & (region_of(level) - 1)) // apart
-            for group in range(sources_of(level) // region_of(level)):
-                for step in far_first(range(count)):
-                    piece = index ^ step
-                    pltpu.make_async_remote_copy(
-                        partial.at[pl.ds(pl.multiple_of(START[level] + piece * rows, 8), rows)],
-                        sums[level].at[pl.ds(pl.multiple_of(place * rows, 8), rows)],
-                        send_sem.at[1],
-                        part_sem.at[level - 1],
-                        device_id=node + group * 32 + first + piece * apart,
-                        device_id_type=LOGICAL,
-                    ).start()
+            index = (place & (sources_of(level) - 1)) // apart
+            for step in far_first(range(count)):
+                piece = index ^ step
+                pltpu.make_async_remote_copy(
+                    partial.at[pl.ds(pl.multiple_of(START[level] + piece * rows, 8), rows)],
+                    sums[level].at[pl.ds(pl.multiple_of(place * rows, 8), rows)],
+                    send_sem.at[1],
+                    part_sem.at[level - 1],
+                    device_id=node + first + piece * apart,
+                    device_id_type=LOGICAL,
+                ).start()
 
     for copy in loads["diag"]:
         copy.wait()
@@ -311,7 +310,7 @@
 
     for level in range(6, 0, -1):
         count, first, apart, rows = OWNERS[level]
-        place = me & (region_of(level) - 1)
+        place = me & (sources_of(level) - 1)
 
         @pl.when(place % apart == first)
         def _(level=level, rows=rows, index=place // apart):
@@ -320,9 +319,9 @@
             total = jnp.sum(sums[level][...].reshape(sources, rows, 128), axis=0)
             rank = ranks[(1 << level) - 2 + (me >> (LEVELS - level))]
             row = lax.broadcasted_iota(jnp.int32, (rows, 128), 0) + index * rows
-            mine = pl.ds(pl.multiple_of(index * rows, 16), rows)
-            got[level][mine, :] = jnp.where(row < rank, total, 0.0).astype(BF16)
-            for step in far_first(range(1, region_of(level))):
+            mine = pl.ds(pl.multiple_of(index * rows, rows), rows)
+            got[level][mine, :] = jnp.where(row < rank, total, 0.0).astype(sum_type(level))
+            for step in far_first(range(1, sources_of(level))):
                 pltpu.make_async_remote_copy(
                     got[level].at[mine],
                     got[level].at[mine],
@@ -335,7 +334,7 @@
     def set_coef(level, values):
         begin = START[level] * 2
         width = WIDTH[level]
-        coef[pl.ds(begin, width), :] = values
+        coef[pl.ds(begin, width), :] = values.astype(BF16)
         coef[pl.ds(begin + width, width), :] = rotated(values.astype(F32)).astype(BF16)
 
     landed(sums[7], 64, part_sem.at[6])
@@ -344,7 +343,7 @@
 
     def await_coef(level):
         count, first, apart, rows = OWNERS[level]
-        owner = (me & (region_of(level) - 1)) % apart == first
+        owner = (me & (sources_of(level) - 1)) % apart == first
 
         @pl.when(owner)
         def _():
@@ -394,13 +393,12 @@
 
     landed(sent, SLOTS - BUCKET, send_sem.at[0])
     landed(partial, TOTAL, send_sem.at[1])
-    landed(partial, WIDTH[1], send_sem.at[1])
     for level in range(1, 7):
         count, first, apart, rows = OWNERS[level]
 
-        @pl.when((me & (region_of(level) - 1)) % apart == first)
+        @pl.when((me & (sources_of(level) - 1)) % apart == first)
         def _(level=level, rows=rows):
-            landed(sent, (region_of(level) - 1) * rows, send_sem.at[2])
+            landed(sent, (sources_of(level) - 1) * max(rows, 16), send_sem.at[2])
 
     for turn, (begin, end) in enumerate(zip(TURNS[:-1], TURNS[1:])):
         count = (end - begin) * BUCKET
@@ -455,7 +453,7 @@
     scratch += [
         pltpu.VMEM(((1 << (LEVELS - level)) * OWNERS[level][3], 128), F32) for level in range(1, 8)
     ]
-    scratch += [pltpu.VMEM((WIDTH[level], 128), BF16) for level in range(1, 7)]
+    scratch += [pltpu.VMEM((WIDTH[level], 128), sum_type(level)) for level in range(1, 7)]
     scratch += [
         pltpu.SemaphoreType.DMA((25,)),
         pltpu.SemaphoreType.DMA((4,)),

time: 46.2 us -> 44.1 us (0.955)
  Pallas kernels: 45.3 us -> 43.1 us
    pallas_call x1, Pallas kernels: 45.3 us -> 43.1 us  [on_device(): pl.pallas_call(body, out_shape=pltpu.VMEM((ROWS, 128), BF16), in_specs=[p...]
where the time goes in v3:
time: 44.1 us; the launch traced here: 44 us
  Pallas kernels  43.1 us (98%)
  other arithmetic  0.83 us (2%)
    pallas_call x1, Pallas kernels, on_device(): pl.pallas_call(body, out_shape=pltpu.VMEM((ROWS, 128), BF16), in_specs=[p...  43.1 us

profile of v3, /device:TPU:1, one launch (start us, length us, event | category | flops | bytes accessed | tf_op | source)
XLA Modules:
  0.0 44.0 jit_solution(8108497982240601340)
XLA Ops:
  0.0 43.1 %tree_product.1 = bf16[1024,128]{1,0:T(8,128)(2,1)S(1)} custom-call(s32[254]{0:T(256)} %ranks_hbm.1, bf16[1024,128]{1,0:T(8,128)(2,1)} %vector_hbm.1, s32[8,128]{1,0:T(8,128)} %bitcast.8, s32[1,128]{1,0:T(1,128)} %bitcast.9, bf16[2,1792,1792]{2,1,0:T(8,128)(2,1)} %diag_hbm.1, bf16[2,2,1792,128]{3,2,1,0:T(8,128)(2,1)} %top_left_hbm.1, ...), custom_call_target="tpu_custom_call" | custom-call | tf_op jit(solution)/shard_map/tree_product/pallas_call | solution.py:464
  43.1 0.8 %convert_element_type.3 = f32[1024,128]{1,0:T(8,128)} convert(bf16[1024,128]{1,0:T(8,128)(2,1)S(1)} %tree_product.1) | non-fusion elementwise | flops 131072 | bytes 786432 | tf_op jit(solution)/shard_map/convert_element_type | solution.py:485

commit v4 on v3

--- a/solution.py
+++ b/solution.py
@@ -259,7 +259,7 @@
 
     landed(arrived, SLOTS - BUCKET, row_sem.at[0])
 
-    wide[...] = arrived[...].astype(F32)
+    wide[pl.ds(0, SLOTS), :] = arrived[...].astype(F32)
     offsets = wide[pl.ds(14, 128, stride=16), :]
     offsets_t = offsets.T
     sub_f = sub.astype(F32)
@@ -279,7 +279,7 @@
             node = ((me >> (LEVELS - level)) ^ 1) << (LEVELS - level)
             place = me & (sources_of(level) - 1)
             index = (place & (sources_of(level) - 1)) // apart
-            for step in far_first(range(count)):
+            for step in sorted(range(count), key=lambda step: -hops(sources_of(level) + step * apart)):
                 piece = index ^ step
                 pltpu.make_async_remote_copy(
                     partial.at[pl.ds(pl.multiple_of(START[level] + piece * rows, 8), rows)],
@@ -378,7 +378,7 @@
         leaving = jnp.dot(put_t[rows, :], field[rows, :], preferred_element_type=F32)
         for half in range(2):
             wide[pl.ds(chunk * 2 + half, 128, stride=16), :] = leaving[half * 128 : half * 128 + 128]
-    returning[...] = wide[...].astype(BF16)
+    returning[...] = wide[pl.ds(0, SLOTS), :].astype(BF16)
     for place, step in enumerate(everyone):
         other = me ^ step
         pltpu.make_async_remote_copy(
@@ -442,7 +442,7 @@
         pltpu.VMEM((CAP, 256), BF16),
         pltpu.VMEM((SLOTS, 128), BF16),
         pltpu.VMEM((SLOTS, 128), BF16),
-        pltpu.VMEM((SLOTS, 128), F32),
+        pltpu.VMEM((SLOTS + BUCKET, 128), F32),
         pltpu.VMEM((2 * CAP, 128), BF16),
         pltpu.VMEM((TOTAL, 128), F32),
         pltpu.VMEM((CAP, 128), F32),

time: 44.1 us -> 44 us (level)
  no operation moved by 1% of the time
where the time goes in v4:
time: 44 us; the launch traced here: 43.9 us
  Pallas kernels  43 us (98%)
  other arithmetic  0.83 us (2%)
    pallas_call x1, Pallas kernels, on_device(): pl.pallas_call(body, out_shape=pltpu.VMEM((ROWS, 128), BF16), in_specs=[p...  43 us

profile of v4, /device:TPU:1, one launch (start us, length us, event | category | flops | bytes accessed | tf_op | source)
XLA Modules:
  0.0 43.9 jit_solution(9703643917192756484)
XLA Ops:
  0.0 43.0 %tree_product.1 = bf16[1024,128]{1,0:T(8,128)(2,1)S(1)} custom-call(s32[254]{0:T(256)} %ranks_hbm.1, bf16[1024,128]{1,0:T(8,128)(2,1)} %vector_hbm.1, s32[8,128]{1,0:T(8,128)} %bitcast.8, s32[1,128]{1,0:T(1,128)} %bitcast.9, bf16[2,1792,1792]{2,1,0:T(8,128)(2,1)} %diag_hbm.1, bf16[2,2,1792,128]{3,2,1,0:T(8,128)(2,1)} %top_left_hbm.1, ...), custom_call_target="tpu_custom_call" | custom-call | tf_op jit(solution)/shard_map/tree_product/pallas_call | solution.py:464
  43.0 0.8 %convert_element_type.3 = f32[1024,128]{1,0:T(8,128)} convert(bf16[1024,128]{1,0:T(8,128)(2,1)S(1)} %tree_product.1) | non-fusion elementwise | flops 131072 | bytes 786432 | tf_op jit(solution)/shard_map/convert_element_type | solution.py:485
